TPU v7x, 512 devices: a whole 4x4x16 slice. The times are simulated.
512 devices in a mesh: section: 32 (over y, x, z_hi), fsdp: 16 (over z_lo, core).
Axes of the slice: x: 4, y: 4, z: 16 (z_hi: 2, z_lo: 8; z = z_hi * 8 + z_lo), core: 2. Of those that a mesh axis runs over, the one named last changes fastest.
Arguments:
- activations: bfloat16 [32, 6144, 2304], P('section', 'fsdp'), may hold values from -6 to 6
- pre_gain: float32 [32, 2304], P('section'), may hold values from 0.5 to 2
- post_gain: float32 [32, 2304], P('section'), may hold values from 0.5 to 2
- w_query: bfloat16 [32, 2304, 1024], P('section', 'fsdp'), may hold values from -2 to 2
- w_keyval: bfloat16 [32, 2304, 1024], P('section', 'fsdp'), may hold values from -0.125 to 0.125
- w_out: bfloat16 [32, 1024, 2304], P('section', 'fsdp'), may hold values from -0.1875 to 0.1875
Outputs:
- advanced: bfloat16 [32, 6144, 2304], P('section', 'fsdp')
All inputs are finite; a program needn't handle non-finite values.
Results may differ from a plain program's by a relative error of at most 0.012.
The roundings to bfloat16 on the way count: a program that leaves them out, or rounds other values in their place, can miss the bound.
Values may be sent and summed in bfloat16 or wider, within the bound.
No kernel may reach another device: no remote copies, remote signals or barrier semaphores. Data moves between devices by JAX's collectives and lax.ppermute only.
A program may use at most 64 MiB of HBM per device.

v0:
```python
import jax
import jax.numpy as jnp
from jax import lax
from jax.sharding import PartitionSpec as P

HEADS = 16
KV_HEADS = 8
HEAD_DIM = 64


def shifted(value, axis, steps):
    count = lax.axis_size(axis)
    pairs = [(source, (source + steps) % count) for source in range(count)]
    return lax.ppermute(value, axis, pairs)


def norm_scale(values, gain):
    mean_square = jnp.mean(values * values, axis=-1, keepdims=True)
    return values * lax.rsqrt(mean_square + 1e-06) * gain


def rotary(heads_in, positions):
    half = heads_in.shape[-1] // 2
    freq = 10000.0 ** (-(jnp.arange(half, dtype=jnp.float32) * 2.0) / heads_in.shape[-1])
    angle = positions[:, None] * freq[None, :]
    cosine = jnp.cos(angle)[:, None, :]
    sine = jnp.sin(angle)[:, None, :]
    first = heads_in[..., :half]
    second = heads_in[..., half:]
    return jnp.concatenate(
        [first * cosine - second * sine, second * cosine + first * sine], axis=-1
    )


def attend(query, keys, values):
    length = query.shape[0]
    group = HEADS // KV_HEADS
    grouped = query.reshape(length, KV_HEADS, group, HEAD_DIM)
    scores = jnp.einsum("skgd,tkd->kgst", grouped, keys, preferred_element_type=jnp.float32)
    capped = 50.0 * jnp.tanh(scores / 50.0)
    causal = jnp.arange(length)[:, None] >= jnp.arange(length)[None, :]
    weights = jnp.where(causal, jnp.exp(capped), 0.0)
    total = jnp.sum(weights, axis=-1, keepdims=True)
    probs = (weights / total).astype(jnp.bfloat16)
    context = jnp.einsum("kgst,tkd->skgd", probs, values, preferred_element_type=jnp.float32)
    return context.reshape(length, HEADS * HEAD_DIM).astype(jnp.bfloat16)


def add_columns(left, piece):
    return jnp.dot(left, piece, preferred_element_type=jnp.float32)


def body(activations, pre_gain, post_gain, w_query, w_keyval, w_out):
    incoming = shifted(activations, "section", 1)[0]
    length = incoming.shape[0]
    widened = incoming.astype(jnp.float32)
    normed = norm_scale(widened, pre_gain[0]).astype(jnp.bfloat16)
    keyval_cols = w_keyval.shape[2]

    def add_one(piece):
        return add_columns(normed, piece)

    qraw = add_one(lax.all_gather(w_query[0], "fsdp", axis=0, tiled=True))
    kvraw = add_one(lax.all_gather(w_keyval[0], "fsdp", axis=0, tiled=True))
    positions = jnp.arange(length, dtype=jnp.float32)
    kv_half = keyval_cols // 2
    query = (rotary(qraw.reshape(length, HEADS, HEAD_DIM), positions) * 144.0 ** (-0.5)).astype(
        jnp.bfloat16
    )
    keys = rotary(kvraw[:, :kv_half].reshape(length, KV_HEADS, HEAD_DIM), positions).astype(
        jnp.bfloat16
    )
    values = kvraw[:, kv_half:].reshape(length, KV_HEADS, HEAD_DIM).astype(jnp.bfloat16)
    context = attend(query, keys, values)
    attended = add_columns(context, lax.all_gather(w_out[0], "fsdp", axis=0, tiled=True))
    advanced = (widened + norm_scale(attended, post_gain[0])).astype(jnp.bfloat16)
    return advanced[None]


def solution(mesh):
    in_specs = (
        P("section", "fsdp", None),
        P("section", None),
        P("section", None),
        P("section", "fsdp", None),
        P("section", "fsdp", None),
        P("section", "fsdp", None),
    )
    out_specs = P("section", "fsdp", None)
    return jax.shard_map(body, mesh=mesh, in_specs=in_specs, out_specs=out_specs, check_vma=False)
```

profile of v0, /device:TPU:1, one launch (start us, length us, event | category | flops | bytes accessed | tf_op | source)
XLA Modules:
  0.0 462.9 jit_solution(11267230818179510200)
XLA Ops:
  6.5 0.0 all-gather.7.cloned.1.call-start
  6.5 0.7 all-gather.7.cloned.1.call-update
  7.3 0.0 all-gather.9.cloned.1.call-start
  7.3 0.7 all-gather.9.cloned.1.call-update
  8.0 0.0 all-gather.11.cloned.1.call-start
  8.1 0.7 all-gather.11.cloned.1.call-update
  8.7 16.3 %collective-permute-start = (bf16[1,384,2304]{2,1,0:T(8,128)(2,1)}, bf16[1,384,2304]{2,1,0:T(8,128)(2,1)S(1)}, u32[]{:S(2)}, u32[]{:S(2)}) collective-permute-start(bf16[1,384,2304]{2,1,0:T(8,128)(2,1)} %param.6), channel_id=1, source_target_pairs={{0,16},{16,32},{32,48},{48,64},{64,80},{80,96},{96,112},{112,128},... | collective-permute-start | bytes 5308424 | tf_op jit(solution)/shard_map/ppermute | solution.py:14
  25.0 0.7 reduce
  25.8 0.7 reduce.1
  26.5 0.7 iota_compare_fusion
  27.2 0.3 fusion.32
  27.5 153.0 %collective-permute-done = bf16[1,384,2304]{2,1,0:T(8,128)(2,1)S(1)} collective-permute-done((bf16[1,384,2304]{2,1,0:T(8,128)(2,1)}, bf16[1,384,2304]{2,1,0:T(8,128)(2,1)S(1)}, u32[]{:S(2)}, u32[]{:S(2)}) %collective-permute-start) | collective-permute-done | bytes 1769504 | tf_op jit(solution)/shard_map/ppermute | solution.py:14
  180.5 0.4 fusion.9
  180.9 53.9 %all-gather.7.cloned.1.call-done = bf16[1,2304,1024]{2,1,0:T(8,128)(2,1)} async-done(((bf16[1,144,1024]{2,1,0:T(8,128)(2,1)}), bf16[1,2304,1024]{2,1,0:T(8,128)(2,1)}) %all-gather.7.cloned.1.call-update) | async-done | bytes 4718608 | tf_op jit(solution)/shard_map/all_gather | solution.py:64
  234.8 4.4 fusion.3
  239.2 0.1 slice.40
  239.2 0.1 slice.26
  239.3 0.9 copy.12
  240.2 101.8 %all-gather.9.cloned.1.call-done = bf16[1,2304,1024]{2,1,0:T(8,128)(2,1)} async-done(((bf16[1,144,1024]{2,1,0:T(8,128)(2,1)}), bf16[1,2304,1024]{2,1,0:T(8,128)(2,1)}) %all-gather.9.cloned.1.call-update) | async-done | bytes 4718608 | tf_op jit(solution)/shard_map/all_gather | solution.py:63
  342.1 6.8 %copy.14 = bf16[1024,2304]{1,0:T(8,128)(2,1)} copy(bf16[1024,2304]{0,1:T(8,128)(2,1)} %bitcast.67) | data formatting | bytes 9437184 | tf_op jit(solution)/shard_map/dot_general | solution.py:50
  348.9 0.3 copy.13
  349.1 0.1 subtract_convert_fusion
  349.3 0.0 copy-start.1
  349.3 4.7 %fusion.16 = f32[384,16,64]{0,2,1:T(8,128)S(1)} fusion(bf16[16,64,2304]{2,1,0:T(8,128)(2,1)} %bitcast.68, bf16[1,384,2304]{2,1,0:T(8,128)(2,1)S(1)} %collective-permute-done, f32[2304]{0:T(1024)S(1)} %reduce, f32[384]{0:T(512)S(1)} %add_rsqrt_fusion.1), kind=kOutput, calls=%fused_computation.21 | convolution fusion | flops 1815478272 | bytes 8071680 | tf_op jit(solution)/shard_map/dot_general | solution.py:50
  354.0 0.2 multiply_subtract_fusion
  354.2 0.0 copy-done.1
  354.2 0.0 copy-start
  354.3 3.1 fusion
  357.4 0.0 copy-done
  357.4 3.5 fusion.25
  360.9 89.1 %all-gather.11.cloned.1.call-done = bf16[1,1024,2304]{2,1,0:T(8,128)(2,1)} async-done(((bf16[1,64,2304]{2,1,0:T(8,128)(2,1)}), bf16[1,1024,2304]{2,1,0:T(8,128)(2,1)}) %all-gather.11.cloned.1.call-update) | async-done | bytes 4718608 | tf_op jit(solution)/shard_map/all_gather | solution.py:75
  449.9 4.5 multiply_reduce_fusion
  454.4 2.0 fusion.18
  (3 shorter events, 0.0 us)
Async XLA Ops:
  6.5 228.3 %all-gather.7.cloned.1.call-start = ((), (), s32[]{:S(2)}) async-start(), calls=%async_computation | async-start | bytes 5013504 | tf_op jit(solution)/shard_map/all_gather | solution.py:64
  7.3 334.8 %all-gather.9.cloned.1.call-start = ((), (), s32[]{:S(2)}) async-start(), calls=%async_computation.1 | async-start | bytes 5013504 | tf_op jit(solution)/shard_map/all_gather | solution.py:63
  8.0 441.9 %all-gather.11.cloned.1.call-start = ((), (), s32[]{:S(2)}) async-start(), calls=%async_computation.2 | async-start | bytes 5013504 | tf_op jit(solution)/shard_map/all_gather | solution.py:75
  8.7 171.8 %collective-permute-start = (bf16[1,384,2304]{2,1,0:T(8,128)(2,1)}, bf16[1,384,2304]{2,1,0:T(8,128)(2,1)S(1)}, u32[]{:S(2)}, u32[]{:S(2)}) collective-permute-start(bf16[1,384,2304]{2,1,0:T(8,128)(2,1)} %param.6), channel_id=1, source_target_pairs={{0,16},{16,32},{32,48},{48,64},{64,80},{80,96},{96,112},{112,128},... | collective-permute-start | bytes 5308424 | tf_op jit(solution)/shard_map/ppermute | solution.py:14
  349.3 5.0 %copy-start.1 = (pred[384,384]{0,1:T(8,128)(4,1)S(1)}, pred[384,384]{0,1:T(8,128)(4,1)}, u32[]{:S(2)}) copy-start(pred[384,384]{0,1:T(8,128)(4,1)} %iota_compare_fusion) | copy-start | bytes 442372
  354.2 3.1 copy-start
Sparse Core Ops, SparseCore 0:
  9.4 225.3 all-gather.6
  236.9 105.1 all-gather.8
  344.1 105.7 all-gather.10
where the time goes:
time: 465 us; the launch traced here: 463 us
  waiting for transfers between devices  400 us (86%)
  matrix products  20.2 us (4%)
  starting transfers between devices  16.3 us (4%)
  between operations  13.2 us (3%)
  local copies, waits for them, and re-layouts  8.11 us (2%)
  other arithmetic  5.18 us (1%)
    ppermute x1, waiting for transfers between devices, shifted(): return lax.ppermute(value, axis, pairs)  153 us
    all_gather x1, waiting for transfers between devices, body(): qraw = add_one(lax.all_gather(w_query[0], 'fsdp', axis=0, tiled=True))  102 us
    all_gather x1, waiting for transfers between devices, body(): lax.all_gather(w_out[0], 'fsdp', axis=0, tiled=True)  89.1 us
    all_gather x1, waiting for transfers between devices, body(): kvraw = add_one(lax.all_gather(w_keyval[0], 'fsdp', axis=0, tiled=True))  53.9 us
    ppermute x1, starting transfers between devices, shifted(): return lax.ppermute(value, axis, pairs)  16.3 us
    dot_general x3, matrix products, add_columns(): return jnp.dot(left, piece, preferred_element_type=jnp.float32)  13.6 us
  transfers between devices with their start and end apart: 4, of which 4 were waited for; matrix products, arithmetic and copies ran while one was open for 6% of the time, Pallas kernels for 0%

commit v1 on v0

v1 whole, which is shorter than its diff:
```python
import jax
import jax.numpy as jnp
from jax import lax
from jax.experimental import pallas as pl
from jax.experimental.pallas import tpu as pltpu
from jax.sharding import PartitionSpec as P

HEAD_DIM = 64
LANES = 128
BLOCK = 128
AXES = ("section", "fsdp")


def moved(value, section_step, flip):
    sections, width = lax.axis_size("section"), lax.axis_size("fsdp")
    pairs = [
        (s * width + f, ((s + section_step) % sections) * width + (f ^ flip))
        for s in range(sections)
        for f in range(width)
    ]
    return lax.ppermute(value, AXES, pairs)


def norm_scale(values, gain):
    mean_square = jnp.mean(values * values, axis=-1, keepdims=True)
    return values * lax.rsqrt(mean_square + 1e-06) * gain


def rotary_tables(length):
    half = HEAD_DIM // 2
    positions = jnp.arange(length, dtype=jnp.float32)
    freq = 10000.0 ** (-(jnp.arange(half, dtype=jnp.float32) * 2.0) / HEAD_DIM)
    angle = positions[:, None] * freq[None, :]
    cosine, sine = jnp.cos(angle), jnp.sin(angle)
    return (
        jnp.concatenate([cosine] * 4, axis=1),
        jnp.concatenate([-sine, sine, -sine, sine], axis=1),
    )


def attention_kernel(raw_ref, cosine_ref, sine_ref, context_ref):
    length = raw_ref.shape[0]
    q_tiles = 2 * context_ref.shape[2] // LANES
    kv_tiles = q_tiles // 2
    lane = lax.broadcasted_iota(jnp.int32, (1, LANES), 1)
    in_first = lane % HEAD_DIM < HEAD_DIM // 2
    low = lane < HEAD_DIM
    cosine, sine = cosine_ref[...], sine_ref[...]

    def tile(index):
        return raw_ref[:, index * LANES : (index + 1) * LANES]

    def rotated(values):
        swapped = jnp.where(
            in_first,
            pltpu.roll(values, LANES - HEAD_DIM // 2, 1),
            pltpu.roll(values, HEAD_DIM // 2, 1),
        )
        return values * cosine + swapped * sine

    def twice(values):
        other = pltpu.roll(values, HEAD_DIM, 1)
        return (
            jnp.where(low, values, other).astype(jnp.bfloat16),
            jnp.where(low, other, values).astype(jnp.bfloat16),
        )

    below = lax.broadcasted_iota(jnp.int32, (BLOCK, BLOCK), 0) >= lax.broadcasted_iota(
        jnp.int32, (BLOCK, BLOCK), 1
    )
    for pair in range(kv_tiles):
        keys = twice(rotated(tile(q_tiles + pair)))
        values = twice(tile(q_tiles + kv_tiles + pair))
        tiles = {}
        for member in range(2):
            at = 2 * pair + member
            query = rotated(tile(at)) * 144.0 ** (-0.5)
            query_low = jnp.where(low, query, 0.0).astype(jnp.bfloat16)
            query_high = jnp.where(low, 0.0, query).astype(jnp.bfloat16)
            for start in range(0, length, BLOCK):
                stop = start + BLOCK
                parts = []
                for part in (query_low, query_high):
                    scores = lax.dot_general(
                        part[start:stop],
                        keys[member][:stop],
                        (((1,), (1,)), ((), ())),
                        preferred_element_type=jnp.float32,
                    )
                    weights = jnp.exp(50.0 * jnp.tanh(scores / 50.0))
                    edge = jnp.where(below, weights[:, start:], 0.0)
                    if start:
                        weights = jnp.concatenate([weights[:, :start], edge], axis=1)
                    else:
                        weights = edge
                    total = jnp.sum(weights, axis=-1, keepdims=True)
                    probs = (weights / total).astype(jnp.bfloat16)
                    parts.append(
                        jnp.dot(probs, values[member][:stop], preferred_element_type=jnp.float32)
                    )
                tiles[member, start] = parts
        for start in range(0, length, BLOCK):
            for parity in range(2):
                context_ref[
                    parity, start : start + BLOCK, pair * LANES : (pair + 1) * LANES
                ] = jnp.where(
                    low, tiles[0, start][parity], tiles[1, start][parity]
                ).astype(jnp.bfloat16)


def half_context(incoming, gain, weights, tables):
    length = incoming.shape[0]
    normed = norm_scale(incoming.astype(jnp.float32), gain).astype(jnp.bfloat16)
    raw = jnp.dot(normed, weights, preferred_element_type=jnp.float32)
    heads_width = weights.shape[1] // 2
    return pl.pallas_call(
        attention_kernel,
        out_shape=jax.ShapeDtypeStruct((2, length, heads_width // 2), jnp.bfloat16),
        compiler_params=pltpu.CompilerParams(vmem_limit_bytes=40 * 1024 * 1024),
        cost_estimate=pl.CostEstimate(
            flops=4 * length * length * heads_width,
            bytes_accessed=length * heads_width * 10,
            transcendentals=2 * length * length * heads_width // HEAD_DIM,
        ),
    )(raw, *tables)


def after(value, *others):
    return lax.optimization_barrier((value, *others))[0]


def body(activations, pre_gain, post_gain, w_query, w_keyval, w_out):
    width = lax.axis_size("fsdp")
    core = lax.axis_index("fsdp") % 2
    core_groups = [list(range(c, width, 2)) for c in range(2)]

    def gather_core(value):
        return lax.all_gather(value, "fsdp", axis=0, axis_index_groups=core_groups)

    incoming = moved(activations[0], 1, 0)
    gathered = gather_core(jnp.concatenate([w_query[0], w_keyval[0]], axis=1))
    out_mine = gather_core(w_out[0])
    gathered, incoming = lax.optimization_barrier((gathered, incoming))
    other = moved(gathered, 0, 1)
    even = jnp.where(core == 0, gathered, other)
    odd = jnp.where(core == 0, other, gathered)
    weights = jnp.stack([even, odd], axis=1).reshape(-1, gathered.shape[-1])
    tables = rotary_tables(incoming.shape[0])
    context = half_context(incoming, pre_gain[0], weights, tables)
    out_mine = after(out_mine, context)
    out_theirs = moved(out_mine, 0, 1)
    attended = jnp.dot(
        jnp.where(core == 0, context[0], context[1]),
        out_mine.reshape(-1, out_mine.shape[-1]),
        preferred_element_type=jnp.float32,
    ) + jnp.dot(
        jnp.where(core == 0, context[1], context[0]),
        out_theirs.reshape(-1, out_theirs.shape[-1]),
        preferred_element_type=jnp.float32,
    )
    advanced = incoming.astype(jnp.float32) + norm_scale(attended, post_gain[0])
    return advanced.astype(jnp.bfloat16)[None]


def solution(mesh):
    in_specs = (
        P("section", "fsdp", None),
        P("section", None),
        P("section", None),
        P("section", "fsdp", None),
        P("section", "fsdp", None),
        P("section", "fsdp", None),
    )
    out_specs = P("section", "fsdp", None)
    return jax.shard_map(body, mesh=mesh, in_specs=in_specs, out_specs=out_specs, check_vma=False)
```

time: 465 us -> 357 us (0.77)
  waiting for transfers between devices: 400 us -> 270 us
  other arithmetic: 5.18 us -> 22.4 us
  Pallas kernels: 0 us -> 13.7 us
  starting transfers between devices: 16.3 us -> 25.2 us
  local copies, waits for them, and re-layouts: 8.11 us -> 0.01 us
  matrix products: 20.2 us -> 12.2 us
    all_gather x3 -> x2, waiting for transfers between devices: 245 us -> 146 us  [gather_core(): return lax.all_gather(value, 'fsdp', axis=0, axis_index_groups=core_groups)]
    ppermute x1 -> x3, waiting for transfers between devices: 153 us -> 124 us  [moved(): return lax.ppermute(value, AXES, pairs)]
    another operation x1 -> x2, other arithmetic: 0.11 us -> 16.3 us  [body(): weights = jnp.stack([even, odd], axis=1).reshape(-1, gathered.shape[-1])]
    pallas_call x0 -> x1, Pallas kernels: none -> 13.7 us  [half_context(): pl.pallas_call(attention_kernel, out_shape=jax.ShapeDtypeStruct((2, lengt...]
    ppermute x1 -> x3, starting transfers between devices: 16.3 us -> 25.1 us  [moved(): return lax.ppermute(value, AXES, pairs)]
    dot_general x5 -> x3, matrix products: 20.2 us -> 12.2 us  [the longest x1 6.46 us: half_context(): raw = jnp.dot(normed, weights, preferred_element_type=jnp.float32)]
    dot_general x1 -> x0, local copies, waits for them, and re-layouts: 6.82 us -> none  [add_columns(): return jnp.dot(left, piece, preferred_element_type=jnp.float32)]
  transfers between devices with their start and end apart: 4 -> 5, of which waited for: 4 -> 5; matrix products, arithmetic and copies ran while one was open for 6% -> 8% of each run, Pallas kernels for 0% -> 4%
where the time goes in v1:
time: 357 us
  waiting for transfers between devices  270 us (76%)
  starting transfers between devices  25.2 us (7%)
  other arithmetic  22.4 us (6%)
  Pallas kernels  13.7 us (4%)
  between operations  13.5 us (4%)
  matrix products  12.2 us (3%)
    all_gather x2, waiting for transfers between devices, gather_core(): return lax.all_gather(value, 'fsdp', axis=0, axis_index_groups=core_groups)  146 us
    ppermute x3, waiting for transfers between devices, moved(): return lax.ppermute(value, AXES, pairs)  124 us
    ppermute x3, starting transfers between devices, moved(): return lax.ppermute(value, AXES, pairs)  25.1 us
    another operation x2, other arithmetic, body(): weights = jnp.stack([even, odd], axis=1).reshape(-1, gathered.shape[-1])  16.3 us
    pallas_call x1, Pallas kernels, half_context(): pl.pallas_call(attention_kernel, out_shape=jax.ShapeDtypeStruct((2, lengt...  13.7 us
  transfers between devices with their start and end apart: 5, of which 5 were waited for; matrix products, arithmetic and copies ran while one was open for 8% of the time, Pallas kernels for 4%

profile of v1, /device:TPU:1, one launch (start us, length us, event | category | flops | bytes accessed | tf_op | source)
XLA Modules:
  0.0 357.0 jit_solution(26584244930374500)
XLA Ops:
  6.5 0.0 all-gather.6.cloned.1.call-start
  6.5 1.9 pad_maximum_fusion.1
  8.4 0.0 all-gather.6.cloned.1.call-update
  8.5 0.0 all-gather.4.cloned.1.call-start
  8.5 16.3 %collective-permute-start = (bf16[384,2304]{1,0:T(8,128)(2,1)}, bf16[384,2304]{1,0:T(8,128)(2,1)S(1)}, u32[]{:S(2)}, u32[]{:S(2)}) collective-permute-start(bf16[384,2304]{1,0:T(8,128)(2,1)} %bitcast.32), channel_id=1, source_target_pairs={{0,16},{1,17},{2,18},{3,19},{4,20},{5,21},{6,22},{7,23},{8,24},{9,... | collective-permute-start | bytes 5308424 | tf_op jit(solution)/shard_map/ppermute | solution.py:21
  24.8 116.9 %collective-permute-done = bf16[384,2304]{1,0:T(8,128)(2,1)S(1)} collective-permute-done((bf16[384,2304]{1,0:T(8,128)(2,1)}, bf16[384,2304]{1,0:T(8,128)(2,1)S(1)}, u32[]{:S(2)}, u32[]{:S(2)}) %collective-permute-start) | collective-permute-done | bytes 1769504 | tf_op jit(solution)/shard_map/ppermute | solution.py:21
  141.7 126.0 %all-gather.6.cloned.1.call-done = bf16[1152,2048]{1,0:T(8,128)(2,1)} async-done(((bf16[144,2048]{1,0:T(8,128)(2,1)}), bf16[1152,2048]{1,0:T(8,128)(2,1)}) %all-gather.6.cloned.1.call-update) | async-done | bytes 4718608 | tf_op jit(solution)/shard_map/all_gather | solution.py:138
  267.6 2.4 collective-permute-start.1
  270.0 0.0 all-gather.4.cloned.1.call-update
  270.1 0.7 reduce
  270.8 0.7 fusion.22
  271.6 0.4 pad_maximum_fusion.2
  271.9 0.4 fusion
  272.4 5.5 %collective-permute-done.1 = bf16[8,144,2048]{2,1,0:T(8,128)(2,1)} collective-permute-done((bf16[8,144,2048]{2,1,0:T(8,128)(2,1)}, bf16[8,144,2048]{2,1,0:T(8,128)(2,1)}, u32[]{:S(2)}, u32[]{:S(2)}) %collective-permute-start.1) | collective-permute-done | bytes 4718624 | tf_op jit(solution)/shard_map/ppermute | solution.py:21
  277.9 8.1 %select_bitcast_fusion.1 = (bf16[8,1,144,2048]{3,2,1,0:T(8,128)(2,1)}, bf16[8,1,144,2048]{3,2,1,0:T(8,128)(2,1)}) fusion(bf16[8,144,2048]{2,1,0:T(8,128)(2,1)} %bitcast.28, bf16[8,144,2048]{2,1,0:T(8,128)(2,1)} %collective-permute-done.1, pred[]{:T(512)S(6)} %eq.4), kind=kLoop, calls=%fused_computation.5 | loop fusion | flops 4718592 | bytes 18874368 | tf_op jit(solution)/shard_map/stack | solution.py:147
  285.9 8.3 %pad_maximum_fusion = bf16[8,2,144,2048]{3,2,1,0:T(8,128)(2,1)} fusion(bf16[8,1,144,2048]{3,2,1,0:T(8,128)(2,1)} %get-tuple-element.12, bf16[8,1,144,2048]{3,2,1,0:T(8,128)(2,1)} %get-tuple-element.11), kind=kLoop, calls=%fused_computation | loop fusion | flops 4718592 | bytes 18874368 | tf_op jit(solution)/shard_map/stack | solution.py:147
  294.2 6.5 %fusion.5.raw_ref = f32[384,2048]{1,0:T(8,128)S(1)} fusion(bf16[2304,2048]{1,0:T(8,128)(2,1)} %bitcast.26, bf16[384,2304]{1,0:T(8,128)(2,1)S(1)} %collective-permute-done, f32[2304]{0:T(1024)S(1)} %reduce, f32[384]{0:T(512)S(1)} %add_rsqrt_fusion.1), kind=kOutput, calls=%fused_computation.13 | convolution fusion | flops 3627417600 | bytes 14363136 | tf_op jit(solution)/shard_map/dot_general | solution.py:114
  300.7 0.0 copy-start
  300.7 13.7 %shard_map.64 = bf16[2,384,512]{2,1,0:T(8,128)(2,1)S(1)} custom-call(f32[384,2048]{1,0:T(8,128)S(1)} %fusion.5.raw_ref, f32[384,128]{1,0:T(8,128)S(1)} %get-tuple-element.18.cosine_ref, f32[384,128]{1,0:T(8,128)S(1)} %get-tuple-element.19.sine_ref), custom_call_target="tpu_custom_call" | custom-call | flops 603979776 | bytes 3932160 | tf_op jit(solution)/shard_map/pallas_call | solution.py:116
  314.4 20.3 %all-gather.4.cloned.1.call-done = bf16[8,64,2304]{2,1,0:T(8,128)(2,1)} async-done(((bf16[1,64,2304]{2,1,0:T(8,128)(2,1)}), bf16[8,64,2304]{2,1,0:T(8,128)(2,1)}) %all-gather.4.cloned.1.call-update) | async-done | bytes 2359312 | tf_op jit(solution)/shard_map/all_gather | solution.py:138
  334.7 6.5 %collective-permute-start.2 = (bf16[8,64,2304]{2,1,0:T(8,128)(2,1)}, bf16[8,64,2304]{2,1,0:T(8,128)(2,1)}, u32[]{:S(2)}, u32[]{:S(2)}) collective-permute-start(bf16[8,64,2304]{2,1,0:T(8,128)(2,1)} %all-gather.4.cloned.1.call-done), channel_id=1, source_target_pairs={{0,1},{1,0},{2,3},{3,2},{4,5},{5,4},{6,7},{7,6},{8,9},{9,8},{10,11... | collective-permute-start | bytes 7077896 | tf_op jit(solution)/shard_map/ppermute | solution.py:21
  341.1 0.0 copy-done
  341.2 2.8 fusion.10
  344.0 1.4 collective-permute-done.2
  345.4 2.9 multiply_reduce_fusion
  348.3 1.9 fusion.4
  (4 shorter events, 0.1 us)
Async XLA Ops:
  6.5 261.1 %all-gather.6.cloned.1.call-start = ((), (), s32[]{:S(2)}) async-start(), calls=%async_computation.1 | async-start | bytes 5308416 | tf_op jit(solution)/shard_map/all_gather | solution.py:138
  8.5 326.2 %all-gather.4.cloned.1.call-start = ((), (), s32[]{:S(2)}) async-start(), calls=%async_computation | async-start | bytes 2654208 | tf_op jit(solution)/shard_map/all_gather | solution.py:138
  8.5 133.1 %collective-permute-start = (bf16[384,2304]{1,0:T(8,128)(2,1)}, bf16[384,2304]{1,0:T(8,128)(2,1)S(1)}, u32[]{:S(2)}, u32[]{:S(2)}) collective-permute-start(bf16[384,2304]{1,0:T(8,128)(2,1)} %bitcast.32), channel_id=1, source_target_pairs={{0,16},{1,17},{2,18},{3,19},{4,20},{5,21},{6,22},{7,23},{8,24},{9,... | collective-permute-start | bytes 5308424 | tf_op jit(solution)/shard_map/ppermute | solution.py:21
  267.6 10.2 %collective-permute-start.1 = (bf16[8,144,2048]{2,1,0:T(8,128)(2,1)}, bf16[8,144,2048]{2,1,0:T(8,128)(2,1)}, u32[]{:S(2)}, u32[]{:S(2)}) collective-permute-start(bf16[8,144,2048]{2,1,0:T(8,128)(2,1)} %bitcast.27), channel_id=1, source_target_pairs={{0,1},{1,0},{2,3},{3,2},{4,5},{5,4},{6,7},{7,6},{8,9},{9,8},{10,11... | collective-permute-start | bytes 14155784 | tf_op jit(solution)/shard_map/ppermute | solution.py:21
  300.7 40.5 %copy-start = (f32[1,2304]{1,0:T(1,128)S(1)}, f32[1,2304]{1,0:T(1,128)}, u32[]{:S(2)}) copy-start(f32[1,2304]{1,0:T(1,128)} %param.8) | copy-start | bytes 27652
  334.7 10.7 %collective-permute-start.2 = (bf16[8,64,2304]{2,1,0:T(8,128)(2,1)}, bf16[8,64,2304]{2,1,0:T(8,128)(2,1)}, u32[]{:S(2)}, u32[]{:S(2)}) collective-permute-start(bf16[8,64,2304]{2,1,0:T(8,128)(2,1)} %all-gather.4.cloned.1.call-done), channel_id=1, source_target_pairs={{0,1},{1,0},{2,3},{3,2},{4,5},{5,4},{6,7},{7,6},{8,9},{9,8},{10,11... | collective-permute-start | bytes 7077896 | tf_op jit(solution)/shard_map/ppermute | solution.py:21
Sparse Core Ops, SparseCore 0:
  9.4 258.1 all-gather.5
  270.2 64.4 all-gather.3

commit v2 on v1

v2 whole, which is shorter than its diff:
```python
import functools

import jax
import jax.numpy as jnp
from jax import lax
from jax.experimental import pallas as pl
from jax.experimental.pallas import tpu as pltpu
from jax.sharding import PartitionSpec as P

HEAD_DIM = 64
LANES = 128
BLOCK = 128
CAP = 50.0
AXES = ("section", "fsdp")


def moved(value, section_step, flip):
    sections, width = lax.axis_size("section"), lax.axis_size("fsdp")
    pairs = [
        (s * width + f, ((s + section_step) % sections) * width + (f ^ flip))
        for s in range(sections)
        for f in range(width)
    ]
    return lax.ppermute(value, AXES, pairs)


def norm_scale(values, gain):
    mean_square = jnp.mean(values * values, axis=-1, keepdims=True)
    return values * lax.rsqrt(mean_square + 1e-06) * gain


def rotary_tables(length):
    half = HEAD_DIM // 2
    positions = jnp.arange(length, dtype=jnp.float32)
    freq = 10000.0 ** (-(jnp.arange(half, dtype=jnp.float32) * 2.0) / HEAD_DIM)
    angle = positions[:, None] * freq[None, :]
    cosine, sine = jnp.cos(angle), jnp.sin(angle)
    return (
        jnp.concatenate([cosine] * 4, axis=1),
        jnp.concatenate([-sine, sine, -sine, sine], axis=1),
    )


def packed(rows, columns):
    count, width = rows.shape
    side = columns // width
    rest = columns - side * width
    deep = count * width // columns
    pieces = [(deep, i * deep, 0, 0, i * width, width) for i in range(side)]
    last = count - side * deep
    pieces += [
        (last, side * deep, at * rest, at * last, side * width, rest)
        for at in range(width // rest)
    ]
    laid = [rows[r : r + n, c : c + m] for n, r, c, _, _, m in pieces]
    tail = jnp.concatenate(laid[side:], axis=0)
    return jnp.concatenate(laid[:side] + [tail], axis=1), pieces


def attention(raw, cosine_ref, sine_ref, store):
    length, width = raw.shape
    q_tiles = width // 2 // LANES
    kv_tiles = q_tiles // 2
    lane = lax.broadcasted_iota(jnp.int32, (1, LANES), 1)
    in_first = lane % HEAD_DIM < HEAD_DIM // 2
    low = lane < HEAD_DIM
    below = lax.broadcasted_iota(jnp.int32, (BLOCK, BLOCK), 0) >= lax.broadcasted_iota(
        jnp.int32, (BLOCK, BLOCK), 1
    )
    below = jnp.concatenate([below, below], axis=0)

    def tile(index):
        return raw[:, index * LANES : (index + 1) * LANES]

    def rotated(values):
        swapped = jnp.where(
            in_first,
            pltpu.roll(values, LANES - HEAD_DIM // 2, 1),
            pltpu.roll(values, HEAD_DIM // 2, 1),
        )
        return values * cosine_ref[...] + swapped * sine_ref[...]

    def twice(values):
        other = pltpu.roll(values, HEAD_DIM, 1)
        return (
            jnp.where(low, values, other).astype(jnp.bfloat16),
            jnp.where(low, other, values).astype(jnp.bfloat16),
        )

    for pair in range(kv_tiles):
        keys = twice(rotated(tile(q_tiles + pair)))
        values = twice(tile(q_tiles + kv_tiles + pair))
        tiles = {}
        for member in range(2):
            query = rotated(tile(2 * pair + member)) * 144.0 ** (-0.5)
            query_low = jnp.where(low, query, 0.0).astype(jnp.bfloat16)
            query_high = jnp.where(low, 0.0, query).astype(jnp.bfloat16)
            for start in range(0, length, BLOCK):
                stop = start + BLOCK
                both = jnp.concatenate([query_low[start:stop], query_high[start:stop]], axis=0)
                scores = lax.dot_general(
                    both,
                    keys[member][:stop],
                    (((1,), (1,)), ((), ())),
                    preferred_element_type=jnp.float32,
                )
                weight = jnp.exp(CAP * jnp.tanh(scores * (1.0 / CAP)))
                edge = jnp.where(below, weight[:, start:], 0.0)
                weight = jnp.concatenate([weight[:, :start], edge], axis=1) if start else edge
                total = jnp.sum(weight, axis=-1, keepdims=True)
                probs = (weight * (1.0 / total)).astype(jnp.bfloat16)
                tiles[member, start] = jnp.dot(
                    probs, values[member][:stop], preferred_element_type=jnp.float32
                )
        for start in range(0, length, BLOCK):
            for parity in range(2):
                part = slice(parity * BLOCK, (parity + 1) * BLOCK)
                store(
                    parity, start, pair, jnp.where(low, tiles[0, start][part], tiles[1, start][part])
                )


def storing(context_ref):
    def store(parity, start, tile, result):
        context_ref[parity, start : start + BLOCK, tile * LANES : (tile + 1) * LANES] = (
            result.astype(jnp.bfloat16)
        )

    return store


def project_kernel(
    pieces, normed_ref, gathered_ref, cosine_ref, sine_ref, context_ref, raw_ref, weights, sems
):
    chips = gathered_ref.shape[0]
    depth = weights.shape[0] // chips
    copies = []
    for chip in range(chips):
        for at, (n, r, c, pr, pc, m) in enumerate(pieces):
            copy = pltpu.make_async_copy(
                gathered_ref.at[chip, pr : pr + n, pc : pc + m],
                weights.at[chip * depth + r : chip * depth + r + n, c : c + m],
                sems.at[chip, at],
            )
            copy.start()
            copies.append(copy)
    length = raw_ref.shape[0]
    half = weights.shape[0] // 2
    split = len(copies) // 2
    for copy in copies[:split]:
        copy.wait()
    raw = jnp.dot(
        normed_ref[length:, :half], weights[:half], preferred_element_type=jnp.float32
    )
    for copy in copies[split:]:
        copy.wait()
    raw += jnp.dot(normed_ref[length:, half:], weights[half:], preferred_element_type=jnp.float32)
    attention(raw, cosine_ref, sine_ref, storing(context_ref))
    raw_ref[...] = jnp.dot(normed_ref[:length, :], weights[...], preferred_element_type=jnp.float32)


def attend_kernel(raw_ref, cosine_ref, sine_ref, context_ref):
    attention(raw_ref[...], cosine_ref, sine_ref, storing(context_ref))


def finish_kernel(
    here_ref, there_ref, mine_ref, theirs_ref, incoming_ref, gain_ref, advanced_ref
):
    core = lax.rem(lax.axis_index("fsdp"), 2)
    depth = here_ref.shape[2]
    own = pl.ds(pl.multiple_of(core * depth, depth), depth)
    got = pl.ds(pl.multiple_of((1 - core) * depth, depth), depth)
    for start in range(0, incoming_ref.shape[0], BLOCK):
        rows = slice(start, start + BLOCK)
        attended = jnp.zeros((BLOCK, incoming_ref.shape[1]), jnp.float32)
        for parity, weights in ((core, mine_ref), (1 - core, theirs_ref)):
            for context_ref, part in ((here_ref, own), (there_ref, got)):
                attended += jnp.dot(
                    context_ref[parity, rows], weights[part, :], preferred_element_type=jnp.float32
                )
        advanced_ref[rows, :] = (
            incoming_ref[rows, :].astype(jnp.float32) + norm_scale(attended, gain_ref[...])
        ).astype(jnp.bfloat16)


def take_kernel(first, gathered_ref, rows_ref, sems):
    chips, last, _ = gathered_ref.shape
    depth = last - first
    copies = [
        pltpu.make_async_copy(
            gathered_ref.at[chip, first:last], rows_ref.at[chip * depth : (chip + 1) * depth], sems.at[chip]
        )
        for chip in range(chips)
    ]
    for copy in copies:
        copy.start()
    for copy in copies:
        copy.wait()


VMEM = pl.BlockSpec(memory_space=pltpu.VMEM)
IN_PLACE = pl.BlockSpec(memory_space=pl.ANY)


def params(megabytes):
    return pltpu.CompilerParams(vmem_limit_bytes=megabytes * 1024 * 1024)


def attention_cost(length, width, depth):
    return pl.CostEstimate(
        flops=4 * length * width * depth + 2 * length * length * width,
        bytes_accessed=2 * (2 * length * depth + depth * width),
        transcendentals=length * length * width // HEAD_DIM,
    )


def body(activations, pre_gain, post_gain, w_query, w_keyval, w_out):
    width = lax.axis_size("fsdp")
    core = lax.axis_index("fsdp") % 2
    core_groups = [list(range(c, width, 2)) for c in range(2)]
    wq, wkv, wo = w_query[0], w_keyval[0], w_out[0]
    q_half, kv_half = wq.shape[1] // 2, wkv.shape[1] // 4

    def columns(side):
        return jnp.concatenate(
            [
                wq[:, side * q_half : (side + 1) * q_half],
                wkv[:, side * kv_half : (side + 1) * kv_half],
                wkv[:, (2 + side) * kv_half : (3 + side) * kv_half],
            ],
            axis=1,
        )

    incoming = moved(activations[0], 1, 0)
    first, second = columns(0), columns(1)
    mine = jnp.where(core == 0, first, second)
    got = moved(jnp.where(core == 0, second, first), 0, 1)
    shards = jnp.concatenate([jnp.where(core == 0, mine, got), jnp.where(core == 0, got, mine)], axis=0)
    shards_packed, pieces = packed(shards, wo.shape[1])
    deep = shards_packed.shape[0]
    gathered = lax.all_gather(
        jnp.concatenate([shards_packed, wo], axis=0), "fsdp", axis=0, axis_index_groups=core_groups
    )
    chips = width // 2
    gathered = gathered.reshape(chips, -1, wo.shape[1])

    normed = norm_scale(incoming.astype(jnp.float32), pre_gain[0]).astype(jnp.bfloat16)
    normed = jnp.concatenate([normed, moved(normed, 0, 1)], axis=0)
    tables = rotary_tables(incoming.shape[0])
    gathered, normed, tables = lax.optimization_barrier((gathered, normed, tables))

    out_mine = pl.pallas_call(
        functools.partial(take_kernel, deep),
        out_shape=jax.ShapeDtypeStruct((chips * wo.shape[0], wo.shape[1]), wo.dtype),
        in_specs=[IN_PLACE],
        out_specs=VMEM,
        scratch_shapes=[pltpu.SemaphoreType.DMA((chips,))],
    )(gathered)
    out_theirs = moved(out_mine, 0, 1)
    length, depth = incoming.shape
    half_width = shards.shape[1]
    context_shape = jax.ShapeDtypeStruct((2, length, half_width // 4), jnp.bfloat16)
    context_away, raw = pl.pallas_call(
        functools.partial(project_kernel, pieces),
        out_shape=(context_shape, jax.ShapeDtypeStruct((length, half_width), jnp.float32)),
        in_specs=[VMEM, IN_PLACE, VMEM, VMEM],
        out_specs=(VMEM, VMEM),
        scratch_shapes=[
            pltpu.VMEM((depth, half_width), jnp.bfloat16),
            pltpu.SemaphoreType.DMA((chips, len(pieces))),
        ],
        compiler_params=params(40),
        cost_estimate=attention_cost(length, half_width, depth),
    )(normed, gathered, *tables)
    there = moved(context_away, 0, 1)
    here = pl.pallas_call(
        attend_kernel,
        out_shape=context_shape,
        in_specs=[VMEM, VMEM, VMEM],
        out_specs=VMEM,
        compiler_params=params(24),
        cost_estimate=attention_cost(length, half_width, 0),
    )(raw, *tables)
    advanced = pl.pallas_call(
        finish_kernel,
        out_shape=jax.ShapeDtypeStruct(incoming.shape, incoming.dtype),
        in_specs=[VMEM] * 6,
        out_specs=VMEM,
        compiler_params=params(32),
        cost_estimate=pl.CostEstimate(
            flops=2 * incoming.size * width * wo.shape[0],
            bytes_accessed=4 * incoming.size + 4 * out_mine.size,
            transcendentals=0,
        ),
    )(here, there, out_mine, out_theirs, incoming, post_gain)
    return advanced[None]


def solution(mesh):
    in_specs = (
        P("section", "fsdp", None),
        P("section", None),
        P("section", None),
        P("section", "fsdp", None),
        P("section", "fsdp", None),
        P("section", "fsdp", None),
    )
    out_specs = P("section", "fsdp", None)
    return jax.shard_map(body, mesh=mesh, in_specs=in_specs, out_specs=out_specs, check_vma=False)
```

time: 357 us -> 353 us (0.989)
  other arithmetic: 22.4 us -> 5.36 us
  matrix products: 12.2 us -> 0 us
  local copies, waits for them, and re-layouts: 0.01 us -> 7.11 us
  waiting for transfers between devices: 270 us -> 277 us
  Pallas kernels: 13.7 us -> 19 us
  starting transfers between devices: 25.2 us -> 30.5 us
    another operation x2 -> x0, other arithmetic: 16.3 us -> none  [body(): weights = jnp.stack([even, odd], axis=1).reshape(-1, gathered.shape[-1])]
    dot_general x3 -> x0, matrix products: 12.2 us -> none  [the longest x1 6.46 us: half_context(): raw = jnp.dot(normed, weights, preferred_element_type=jnp.float32)]
    ppermute x3 -> x5, waiting for transfers between devices: 124 us -> 132 us  [moved(): return lax.ppermute(value, AXES, pairs)]
    ppermute x3 -> x5, starting transfers between devices: 25.1 us -> 30.5 us  [moved(): return lax.ppermute(value, AXES, pairs)]
    pallas_call x1 -> x4, Pallas kernels: 13.7 us -> 19 us  [the longest x1 8.13 us: body(): pl.pallas_call(functools.partial(project_kernel, pieces), out_shape=(cont...]
    unnamed x2 -> x12, local copies, waits for them, and re-layouts: 0.01 us -> 5.03 us
    all_gather x2 -> x1, waiting for transfers between devices: 146 us -> 145 us  [body(): lax.all_gather(jnp.concatenate([shards_packed, wo], axis=0), 'fsdp', axis...]
  transfers between devices with their start and end apart: 5 -> 6, of which waited for: 5 -> 4; matrix products, arithmetic and copies ran while one was open for 8% -> 1% of each run, Pallas kernels for 4% -> 3%
where the time goes in v2:
time: 353 us
  waiting for transfers between devices  277 us (78%)
  starting transfers between devices  30.5 us (9%)
  Pallas kernels  19 us (5%)
  between operations  13.6 us (4%)
  local copies, waits for them, and re-layouts  7.11 us (2%)
  other arithmetic  5.36 us (2%)
    all_gather x1, waiting for transfers between devices, body(): lax.all_gather(jnp.concatenate([shards_packed, wo], axis=0), 'fsdp', axis...  145 us
    ppermute x5, waiting for transfers between devices, moved(): return lax.ppermute(value, AXES, pairs)  132 us
    ppermute x5, starting transfers between devices, moved(): return lax.ppermute(value, AXES, pairs)  30.5 us
    pallas_call x1, Pallas kernels, body(): pl.pallas_call(functools.partial(project_kernel, pieces), out_shape=(cont...  8.13 us
  transfers between devices with their start and end apart: 6, of which 4 were waited for; matrix products, arithmetic and copies ran while one was open for 1% of the time, Pallas kernels for 3%

profile of v2, /device:TPU:1, one launch (start us, length us, event | category | flops | bytes accessed | tf_op | source)
XLA Modules:
  0.0 352.5 jit_solution(16102140813321056789)
XLA Ops:
  6.5 0.0 all-gather.3.cloned.1.call-start
  6.5 1.0 fusion.16
  7.6 0.0 copy-start.4
  7.6 1.0 fusion.15
  8.6 0.1 broadcast_select_fusion.2
  8.7 8.8 %collective-permute-start = (bf16[144,1024]{1,0:T(8,128)(2,1)S(1)}, bf16[144,1024]{1,0:T(8,128)(2,1)S(1)}, u32[]{:S(2)}, u32[]{:S(2)}) collective-permute-start(bf16[144,1024]{1,0:T(8,128)(2,1)S(1)} %broadcast_select_fusion.2), channel_id=1, source_target_pairs={{0,1},{1,0},{2,3},{3,2},{4,5},{5,4},{6,7},{7,6},{8,9},{9,8},{10,11... | collective-permute-start | bytes 884744 | tf_op jit(solution)/shard_map/ppermute | solution.py:24
  17.5 1.2 collective-permute-done
  18.7 0.1 broadcast_select_fusion.1
  18.8 0.0 copy-start.5
  18.9 0.0 copy-done.4
  18.9 1.0 fusion.10
  19.9 0.0 all-gather.3.cloned.1.call-update
  19.9 10.1 %collective-permute-start.1 = (bf16[384,2304]{1,0:T(8,128)(2,1)}, bf16[384,2304]{1,0:T(8,128)(2,1)S(1)}, u32[]{:S(2)}, u32[]{:S(2)}) collective-permute-start(bf16[384,2304]{1,0:T(8,128)(2,1)} %bitcast.4), channel_id=1, source_target_pairs={{0,16},{1,17},{2,18},{3,19},{4,20},{5,21},{6,22},{7,23},{8,24},{9,... | collective-permute-start | bytes 5308424 | tf_op jit(solution)/shard_map/ppermute | solution.py:24
  30.0 0.0 copy-done.5
  30.0 128.3 %collective-permute-done.1.incoming_ref = bf16[384,2304]{1,0:T(8,128)(2,1)S(1)} collective-permute-done((bf16[384,2304]{1,0:T(8,128)(2,1)}, bf16[384,2304]{1,0:T(8,128)(2,1)S(1)}, u32[]{:S(2)}, u32[]{:S(2)}) %collective-permute-start.1) | collective-permute-done | bytes 1769504 | tf_op jit(solution)/shard_map/ppermute | solution.py:24
  158.3 0.4 fusion
  158.7 0.5 fusion.2
  159.2 7.1 %collective-permute-start.2 = (bf16[384,2304]{1,0:T(8,128)(2,1)S(1)}, bf16[384,2304]{1,0:T(8,128)(2,1)S(1)}, u32[]{:S(2)}, u32[]{:S(2)}) collective-permute-start(bf16[384,2304]{1,0:T(8,128)(2,1)S(1)} %fusion.2), channel_id=1, source_target_pairs={{0,1},{1,0},{2,3},{3,2},{4,5},{5,4},{6,7},{7,6},{8,9},{9,8},{10,11... | collective-permute-start | bytes 5308424 | tf_op jit(solution)/shard_map/ppermute | solution.py:24
  166.4 0.7 fusion.13
  167.1 0.4 pad_maximum_fusion.3
  167.5 2.2 collective-permute-done.2
  169.7 2.1 pad_maximum_fusion.normed_ref
  171.8 145.3 %all-gather.3.cloned.1.call-done = bf16[1536,2304]{1,0:T(8,128)(2,1)} async-done(((bf16[192,2304]{1,0:T(8,128)(2,1)}), bf16[1536,2304]{1,0:T(8,128)(2,1)}) %all-gather.3.cloned.1.call-update) | async-done | bytes 7077904 | tf_op jit(solution)/shard_map/all_gather | solution.py:241
  317.0 3.1 shard_map.66.mine_ref
  320.1 2.4 collective-permute-start.4
  322.5 0.0 copy-start.1
  322.6 3.0 copy-done.1
  325.6 0.0 copy-start.2
  325.6 2.0 copy-done.2
  327.6 8.1 %shard_map.64 = (bf16[2,384,256]{2,1,0:T(8,128)(2,1)S(1)}, f32[384,1024]{1,0:T(8,128)S(1)}) custom-call(bf16[768,2304]{1,0:T(8,128)(2,1)S(1)} %copy-done.2, bf16[8,192,2304]{2,1,0:T(8,128)(2,1)S(1)} %bitcast.7, f32[384,128]{1,0:T(8,128)S(1)} %get-tuple-element.13.cosine_ref, f32[384,128]{1,0:T(8,128)S(1)} %get-tuple-element.14.sine_ref), custom_call_target="tpu_custom_call" | custom-call | flops 3925868544 | bytes 8257536 | tf_op jit(solution)/shard_map/pallas_call | solution.py:263
  335.7 2.1 collective-permute-start.3
  337.8 0.0 copy-start
  337.8 0.0 copy-start.3
  337.8 3.9 %shard_map.65.here_ref = bf16[2,384,256]{2,1,0:T(8,128)(2,1)S(1)} custom-call(f32[384,1024]{1,0:T(8,128)S(1)} %get-tuple-element.15.raw_ref, f32[384,128]{1,0:T(8,128)S(1)} %get-tuple-element.13.cosine_ref, f32[384,128]{1,0:T(8,128)S(1)} %get-tuple-element.14.sine_ref), custom_call_target="tpu_custom_call" | custom-call | flops 301989888 | tf_op jit(solution)/shard_map/pallas_call | solution.py:276
  341.8 0.0 collective-permute-done.3.there_ref
  341.8 0.0 collective-permute-done.4.theirs_ref
  341.8 0.0 copy-done
  341.8 0.0 copy-done.3
  341.8 3.9 %shard_map.67 = bf16[384,2304]{1,0:T(8,128)(2,1)} custom-call(bf16[2,384,256]{2,1,0:T(8,128)(2,1)S(1)} %shard_map.65.here_ref, bf16[2,384,256]{2,1,0:T(8,128)(2,1)S(1)} %collective-permute-done.3.there_ref, bf16[512,2304]{1,0:T(8,128)(2,1)S(1)} %copy-done, bf16[512,2304]{1,0:T(8,128)(2,1)S(1)} %collective-permute-done.4.theirs_ref, ...), custom_call_target="tpu_custom_call" | custom-call | flops 1811939328 | bytes 8257536 | tf_op jit(solution)/shard_map/pallas_call | solution.py:284
  (5 shorter events, 0.1 us)
Async XLA Ops:
  6.5 310.5 %all-gather.3.cloned.1.call-start = ((), (), s32[]{:S(2)}) async-start(), calls=%async_computation | async-start | bytes 7962624 | tf_op jit(solution)/shard_map/all_gather | solution.py:241
  7.6 11.3 %copy-start.4 = (bf16[1,64,2304]{2,1,0:T(8,128)(2,1)S(1)}, bf16[1,64,2304]{2,1,0:T(8,128)(2,1)}, u32[]{:S(2)}) copy-start(bf16[1,64,2304]{2,1,0:T(8,128)(2,1)} %param.11) | copy-start | bytes 884740
  8.7 10.0 %collective-permute-start = (bf16[144,1024]{1,0:T(8,128)(2,1)S(1)}, bf16[144,1024]{1,0:T(8,128)(2,1)S(1)}, u32[]{:S(2)}, u32[]{:S(2)}) collective-permute-start(bf16[144,1024]{1,0:T(8,128)(2,1)S(1)} %broadcast_select_fusion.2), channel_id=1, source_target_pairs={{0,1},{1,0},{2,3},{3,2},{4,5},{5,4},{6,7},{7,6},{8,9},{9,8},{10,11... | collective-permute-start | bytes 884744 | tf_op jit(solution)/shard_map/ppermute | solution.py:24
  18.8 11.1 %copy-start.5 = (f32[1,2304]{1,0:T(1,128)S(1)}, f32[1,2304]{1,0:T(1,128)}, u32[]{:S(2)}) copy-start(f32[1,2304]{1,0:T(1,128)} %param.7) | copy-start | bytes 27652
  19.9 138.4 %collective-permute-start.1 = (bf16[384,2304]{1,0:T(8,128)(2,1)}, bf16[384,2304]{1,0:T(8,128)(2,1)S(1)}, u32[]{:S(2)}, u32[]{:S(2)}) collective-permute-start(bf16[384,2304]{1,0:T(8,128)(2,1)} %bitcast.4), channel_id=1, source_target_pairs={{0,16},{1,17},{2,18},{3,19},{4,20},{5,21},{6,22},{7,23},{8,24},{9,... | collective-permute-start | bytes 5308424 | tf_op jit(solution)/shard_map/ppermute | solution.py:24
  159.2 10.4 %collective-permute-start.2 = (bf16[384,2304]{1,0:T(8,128)(2,1)S(1)}, bf16[384,2304]{1,0:T(8,128)(2,1)S(1)}, u32[]{:S(2)}, u32[]{:S(2)}) collective-permute-start(bf16[384,2304]{1,0:T(8,128)(2,1)S(1)} %fusion.2), channel_id=1, source_target_pairs={{0,1},{1,0},{2,3},{3,2},{4,5},{5,4},{6,7},{7,6},{8,9},{9,8},{10,11... | collective-permute-start | bytes 5308424 | tf_op jit(solution)/shard_map/ppermute | solution.py:24
  320.1 21.6 %collective-permute-start.4 = (bf16[512,2304]{1,0:T(8,128)(2,1)}, bf16[512,2304]{1,0:T(8,128)(2,1)S(1)}, u32[]{:S(2)}, u32[]{:S(2)}) collective-permute-start(bf16[512,2304]{1,0:T(8,128)(2,1)} %shard_map.66.mine_ref), channel_id=1, source_target_pairs={{0,1},{1,0},{2,3},{3,2},{4,5},{5,4},{6,7},{7,6},{8,9},{9,8},{10,11... | collective-permute-start | bytes 7077896 | tf_op jit(solution)/shard_map/ppermute | solution.py:24
  322.5 3.0 copy-start.1
  325.6 2.0 copy-start.2
  335.7 6.1 %collective-permute-start.3 = (bf16[2,384,256]{2,1,0:T(8,128)(2,1)S(1)}, bf16[2,384,256]{2,1,0:T(8,128)(2,1)S(1)}, u32[]{:S(2)}, u32[]{:S(2)}) collective-permute-start(bf16[2,384,256]{2,1,0:T(8,128)(2,1)S(1)} %get-tuple-element.16), channel_id=1, source_target_pairs={{0,1},{1,0},{2,3},{3,2},{4,5},{5,4},{6,7},{7,6},{8,9},{9,8},{10,11... | collective-permute-start | bytes 1179656 | tf_op jit(solution)/shard_map/ppermute | solution.py:24
  337.8 4.0 %copy-start = (bf16[512,2304]{1,0:T(8,128)(2,1)S(1)}, bf16[512,2304]{1,0:T(8,128)(2,1)}, u32[]{:S(2)}) copy-start(bf16[512,2304]{1,0:T(8,128)(2,1)} %shard_map.66.mine_ref) | copy-start | bytes 7077892
  337.8 4.0 %copy-start.3 = (f32[1,2304]{1,0:T(1,128)S(1)}, f32[1,2304]{1,0:T(1,128)}, u32[]{:S(2)}) copy-start(f32[1,2304]{1,0:T(1,128)} %gain_ref.1) | copy-start | bytes 27652
Sparse Core Ops, SparseCore 0:
  20.0 296.9 all-gather.2

commit v3 on v2

--- a/solution.py
+++ b/solution.py
@@ -269,7 +269,7 @@
             pltpu.VMEM((depth, half_width), jnp.bfloat16),
             pltpu.SemaphoreType.DMA((chips, len(pieces))),
         ],
-        compiler_params=params(40),
+        compiler_params=params(48),
         cost_estimate=attention_cost(length, half_width, depth),
     )(normed, gathered, *tables)
     there = moved(context_away, 0, 1)

time: 353 us -> 351 us (level)
  transfers between devices with their start and end apart: 6 -> 6, of which waited for: 4 -> 4; matrix products, arithmetic and copies ran while one was open for 1% -> 1% of each run, Pallas kernels for 3% -> 4%
where the time goes in v3:
time: 351 us
  waiting for transfers between devices  277 us (79%)
  starting transfers between devices  30.5 us (9%)
  Pallas kernels  20.6 us (6%)
  between operations  13.6 us (4%)
  other arithmetic  5.35 us (2%)
  local copies, waits for them, and re-layouts  4.11 us (1%)
    all_gather x1, waiting for transfers between devices, body(): lax.all_gather(jnp.concatenate([shards_packed, wo], axis=0), 'fsdp', axis...  145 us
    ppermute x5, waiting for transfers between devices, moved(): return lax.ppermute(value, AXES, pairs)  132 us
    ppermute x5, starting transfers between devices, moved(): return lax.ppermute(value, AXES, pairs)  30.5 us
    pallas_call x1, Pallas kernels, body(): pl.pallas_call(functools.partial(project_kernel, pieces), out_shape=(cont...  9.73 us
  transfers between devices with their start and end apart: 6, of which 4 were waited for; matrix products, arithmetic and copies ran while one was open for 1% of the time, Pallas kernels for 4%

profile of v3, /device:TPU:1, one launch (start us, length us, event | category | flops | bytes accessed | tf_op | source)
XLA Modules:
  0.0 351.1 jit_solution(764626764438923673)
XLA Ops:
  6.5 0.0 all-gather.3.cloned.1.call-start
  6.5 1.0 fusion.16
  7.6 0.0 copy-start.3
  7.6 1.0 fusion.15
  8.6 0.1 broadcast_select_fusion.2
  8.7 8.8 %collective-permute-start = (bf16[144,1024]{1,0:T(8,128)(2,1)S(1)}, bf16[144,1024]{1,0:T(8,128)(2,1)S(1)}, u32[]{:S(2)}, u32[]{:S(2)}) collective-permute-start(bf16[144,1024]{1,0:T(8,128)(2,1)S(1)} %broadcast_select_fusion.2), channel_id=1, source_target_pairs={{0,1},{1,0},{2,3},{3,2},{4,5},{5,4},{6,7},{7,6},{8,9},{9,8},{10,11... | collective-permute-start | bytes 884744 | tf_op jit(solution)/shard_map/ppermute | solution.py:24
  17.5 1.2 collective-permute-done
  18.7 0.1 broadcast_select_fusion.1
  18.8 0.0 copy-start.4
  18.9 0.0 copy-done.3
  18.9 1.0 fusion.10
  19.9 0.0 all-gather.3.cloned.1.call-update
  19.9 10.1 %collective-permute-start.1 = (bf16[384,2304]{1,0:T(8,128)(2,1)}, bf16[384,2304]{1,0:T(8,128)(2,1)S(1)}, u32[]{:S(2)}, u32[]{:S(2)}) collective-permute-start(bf16[384,2304]{1,0:T(8,128)(2,1)} %bitcast.4), channel_id=1, source_target_pairs={{0,16},{1,17},{2,18},{3,19},{4,20},{5,21},{6,22},{7,23},{8,24},{9,... | collective-permute-start | bytes 5308424 | tf_op jit(solution)/shard_map/ppermute | solution.py:24
  30.0 0.0 copy-done.4
  30.0 128.3 %collective-permute-done.1.incoming_ref = bf16[384,2304]{1,0:T(8,128)(2,1)S(1)} collective-permute-done((bf16[384,2304]{1,0:T(8,128)(2,1)}, bf16[384,2304]{1,0:T(8,128)(2,1)S(1)}, u32[]{:S(2)}, u32[]{:S(2)}) %collective-permute-start.1) | collective-permute-done | bytes 1769504 | tf_op jit(solution)/shard_map/ppermute | solution.py:24
  158.3 0.4 fusion
  158.7 0.5 fusion.2
  159.2 7.1 %collective-permute-start.2 = (bf16[384,2304]{1,0:T(8,128)(2,1)S(1)}, bf16[384,2304]{1,0:T(8,128)(2,1)S(1)}, u32[]{:S(2)}, u32[]{:S(2)}) collective-permute-start(bf16[384,2304]{1,0:T(8,128)(2,1)S(1)} %fusion.2), channel_id=1, source_target_pairs={{0,1},{1,0},{2,3},{3,2},{4,5},{5,4},{6,7},{7,6},{8,9},{9,8},{10,11... | collective-permute-start | bytes 5308424 | tf_op jit(solution)/shard_map/ppermute | solution.py:24
  166.4 0.7 fusion.13
  167.1 0.4 pad_maximum_fusion.3
  167.5 2.2 collective-permute-done.2
  169.7 2.1 pad_maximum_fusion.normed_ref
  171.7 145.3 %all-gather.3.cloned.1.call-done = bf16[1536,2304]{1,0:T(8,128)(2,1)} async-done(((bf16[192,2304]{1,0:T(8,128)(2,1)}), bf16[1536,2304]{1,0:T(8,128)(2,1)}) %all-gather.3.cloned.1.call-update) | async-done | bytes 7077904 | tf_op jit(solution)/shard_map/all_gather | solution.py:241
  317.0 3.1 shard_map.66.mine_ref
  320.1 2.4 collective-permute-start.4
  322.5 0.0 copy-start.1
  322.5 2.0 copy-done.1
  324.5 9.7 %shard_map.64 = (bf16[2,384,256]{2,1,0:T(8,128)(2,1)S(1)}, f32[384,1024]{1,0:T(8,128)S(1)}) custom-call(bf16[768,2304]{1,0:T(8,128)(2,1)S(1)} %copy-done.1, bf16[8,192,2304]{2,1,0:T(8,128)(2,1)} %bitcast.7, f32[384,128]{1,0:T(8,128)S(1)} %get-tuple-element.13.cosine_ref, f32[384,128]{1,0:T(8,128)S(1)} %get-tuple-element.14.sine_ref), custom_call_target="tpu_custom_call" | custom-call | flops 3925868544 | bytes 8257536 | tf_op jit(solution)/shard_map/pallas_call | solution.py:263
  334.3 2.1 collective-permute-start.3
  336.4 0.0 copy-start
  336.4 0.0 copy-start.2
  336.4 3.9 %shard_map.65.here_ref = bf16[2,384,256]{2,1,0:T(8,128)(2,1)S(1)} custom-call(f32[384,1024]{1,0:T(8,128)S(1)} %get-tuple-element.15.raw_ref, f32[384,128]{1,0:T(8,128)S(1)} %get-tuple-element.13.cosine_ref, f32[384,128]{1,0:T(8,128)S(1)} %get-tuple-element.14.sine_ref), custom_call_target="tpu_custom_call" | custom-call | flops 301989888 | tf_op jit(solution)/shard_map/pallas_call | solution.py:276
  340.4 0.0 collective-permute-done.3.there_ref
  340.4 0.0 collective-permute-done.4.theirs_ref
  340.4 0.0 copy-done
  340.4 0.0 copy-done.2
  340.4 3.9 %shard_map.67 = bf16[384,2304]{1,0:T(8,128)(2,1)} custom-call(bf16[2,384,256]{2,1,0:T(8,128)(2,1)S(1)} %shard_map.65.here_ref, bf16[2,384,256]{2,1,0:T(8,128)(2,1)S(1)} %collective-permute-done.3.there_ref, bf16[512,2304]{1,0:T(8,128)(2,1)S(1)} %copy-done, bf16[512,2304]{1,0:T(8,128)(2,1)S(1)} %collective-permute-done.4.theirs_ref, ...), custom_call_target="tpu_custom_call" | custom-call | flops 1811939328 | bytes 8257536 | tf_op jit(solution)/shard_map/pallas_call | solution.py:284
  (5 shorter events, 0.1 us)
Async XLA Ops:
  6.5 310.5 %all-gather.3.cloned.1.call-start = ((), (), s32[]{:S(2)}) async-start(), calls=%async_computation | async-start | bytes 7962624 | tf_op jit(solution)/shard_map/all_gather | solution.py:241
  7.6 11.3 %copy-start.3 = (bf16[1,64,2304]{2,1,0:T(8,128)(2,1)S(1)}, bf16[1,64,2304]{2,1,0:T(8,128)(2,1)}, u32[]{:S(2)}) copy-start(bf16[1,64,2304]{2,1,0:T(8,128)(2,1)} %param.11) | copy-start | bytes 884740
  8.7 10.0 %collective-permute-start = (bf16[144,1024]{1,0:T(8,128)(2,1)S(1)}, bf16[144,1024]{1,0:T(8,128)(2,1)S(1)}, u32[]{:S(2)}, u32[]{:S(2)}) collective-permute-start(bf16[144,1024]{1,0:T(8,128)(2,1)S(1)} %broadcast_select_fusion.2), channel_id=1, source_target_pairs={{0,1},{1,0},{2,3},{3,2},{4,5},{5,4},{6,7},{7,6},{8,9},{9,8},{10,11... | collective-permute-start | bytes 884744 | tf_op jit(solution)/shard_map/ppermute | solution.py:24
  18.8 11.1 %copy-start.4 = (f32[1,2304]{1,0:T(1,128)S(1)}, f32[1,2304]{1,0:T(1,128)}, u32[]{:S(2)}) copy-start(f32[1,2304]{1,0:T(1,128)} %param.7) | copy-start | bytes 27652
  19.9 138.4 %collective-permute-start.1 = (bf16[384,2304]{1,0:T(8,128)(2,1)}, bf16[384,2304]{1,0:T(8,128)(2,1)S(1)}, u32[]{:S(2)}, u32[]{:S(2)}) collective-permute-start(bf16[384,2304]{1,0:T(8,128)(2,1)} %bitcast.4), channel_id=1, source_target_pairs={{0,16},{1,17},{2,18},{3,19},{4,20},{5,21},{6,22},{7,23},{8,24},{9,... | collective-permute-start | bytes 5308424 | tf_op jit(solution)/shard_map/ppermute | solution.py:24
  159.2 10.4 %collective-permute-start.2 = (bf16[384,2304]{1,0:T(8,128)(2,1)S(1)}, bf16[384,2304]{1,0:T(8,128)(2,1)S(1)}, u32[]{:S(2)}, u32[]{:S(2)}) collective-permute-start(bf16[384,2304]{1,0:T(8,128)(2,1)S(1)} %fusion.2), channel_id=1, source_target_pairs={{0,1},{1,0},{2,3},{3,2},{4,5},{5,4},{6,7},{7,6},{8,9},{9,8},{10,11... | collective-permute-start | bytes 5308424 | tf_op jit(solution)/shard_map/ppermute | solution.py:24
  320.1 20.2 %collective-permute-start.4 = (bf16[512,2304]{1,0:T(8,128)(2,1)}, bf16[512,2304]{1,0:T(8,128)(2,1)S(1)}, u32[]{:S(2)}, u32[]{:S(2)}) collective-permute-start(bf16[512,2304]{1,0:T(8,128)(2,1)} %shard_map.66.mine_ref), channel_id=1, source_target_pairs={{0,1},{1,0},{2,3},{3,2},{4,5},{5,4},{6,7},{7,6},{8,9},{9,8},{10,11... | collective-permute-start | bytes 7077896 | tf_op jit(solution)/shard_map/ppermute | solution.py:24
  322.5 2.0 copy-start.1
  334.3 6.1 %collective-permute-start.3 = (bf16[2,384,256]{2,1,0:T(8,128)(2,1)S(1)}, bf16[2,384,256]{2,1,0:T(8,128)(2,1)S(1)}, u32[]{:S(2)}, u32[]{:S(2)}) collective-permute-start(bf16[2,384,256]{2,1,0:T(8,128)(2,1)S(1)} %get-tuple-element.16), channel_id=1, source_target_pairs={{0,1},{1,0},{2,3},{3,2},{4,5},{5,4},{6,7},{7,6},{8,9},{9,8},{10,11... | collective-permute-start | bytes 1179656 | tf_op jit(solution)/shard_map/ppermute | solution.py:24
  336.4 4.0 %copy-start = (bf16[512,2304]{1,0:T(8,128)(2,1)S(1)}, bf16[512,2304]{1,0:T(8,128)(2,1)}, u32[]{:S(2)}) copy-start(bf16[512,2304]{1,0:T(8,128)(2,1)} %shard_map.66.mine_ref) | copy-start | bytes 7077892
  336.4 4.0 %copy-start.2 = (f32[1,2304]{1,0:T(1,128)S(1)}, f32[1,2304]{1,0:T(1,128)}, u32[]{:S(2)}) copy-start(f32[1,2304]{1,0:T(1,128)} %gain_ref.1) | copy-start | bytes 27652
Sparse Core Ops, SparseCore 0:
  20.0 296.9 all-gather.2

commit v4 on v3

--- a/solution.py
+++ b/solution.py
@@ -152,11 +152,16 @@
     raw = jnp.dot(
         normed_ref[length:, :half], weights[:half], preferred_element_type=jnp.float32
     )
+    raw_ref[...] = jnp.dot(
+        normed_ref[:length, :half], weights[:half], preferred_element_type=jnp.float32
+    )
     for copy in copies[split:]:
         copy.wait()
     raw += jnp.dot(normed_ref[length:, half:], weights[half:], preferred_element_type=jnp.float32)
     attention(raw, cosine_ref, sine_ref, storing(context_ref))
-    raw_ref[...] = jnp.dot(normed_ref[:length, :], weights[...], preferred_element_type=jnp.float32)
+    raw_ref[...] += jnp.dot(
+        normed_ref[:length, half:], weights[half:], preferred_element_type=jnp.float32
+    )
 
 
 def attend_kernel(raw_ref, cosine_ref, sine_ref, context_ref):

time: 351 us -> 351 us (level)
  no operation moved by 1% of the time
where the time goes in v4:
time: 351 us
  waiting for transfers between devices  277 us (79%)
  starting transfers between devices  30.5 us (9%)
  Pallas kernels  20.3 us (6%)
  between operations  13.6 us (4%)
  other arithmetic  5.35 us (2%)
  local copies, waits for them, and re-layouts  4.11 us (1%)
    all_gather x1, waiting for transfers between devices, body(): lax.all_gather(jnp.concatenate([shards_packed, wo], axis=0), 'fsdp', axis...  145 us
    ppermute x5, waiting for transfers between devices, moved(): return lax.ppermute(value, AXES, pairs)  132 us
    ppermute x5, starting transfers between devices, moved(): return lax.ppermute(value, AXES, pairs)  30.5 us
    pallas_call x1, Pallas kernels, body(): pl.pallas_call(functools.partial(project_kernel, pieces), out_shape=(cont...  9.46 us
  transfers between devices with their start and end apart: 6, of which 4 were waited for; matrix products, arithmetic and copies ran while one was open for 1% of the time, Pallas kernels for 4%

profile of v4, /device:TPU:1, one launch (start us, length us, event | category | flops | bytes accessed | tf_op | source)
XLA Modules:
  0.0 350.8 jit_solution(12138206781244915138)
XLA Ops:
  6.5 0.0 all-gather.3.cloned.1.call-start
  6.5 1.0 fusion.16
  7.6 0.0 copy-start.3
  7.6 1.0 fusion.15
  8.6 0.1 broadcast_select_fusion.2
  8.7 8.8 %collective-permute-start = (bf16[144,1024]{1,0:T(8,128)(2,1)S(1)}, bf16[144,1024]{1,0:T(8,128)(2,1)S(1)}, u32[]{:S(2)}, u32[]{:S(2)}) collective-permute-start(bf16[144,1024]{1,0:T(8,128)(2,1)S(1)} %broadcast_select_fusion.2), channel_id=1, source_target_pairs={{0,1},{1,0},{2,3},{3,2},{4,5},{5,4},{6,7},{7,6},{8,9},{9,8},{10,11... | collective-permute-start | bytes 884744 | tf_op jit(solution)/shard_map/ppermute | solution.py:24
  17.5 1.2 collective-permute-done
  18.7 0.1 broadcast_select_fusion.1
  18.8 0.0 copy-start.4
  18.9 0.0 copy-done.3
  18.9 1.0 fusion.10
  19.9 0.0 all-gather.3.cloned.1.call-update
  19.9 10.1 %collective-permute-start.1 = (bf16[384,2304]{1,0:T(8,128)(2,1)}, bf16[384,2304]{1,0:T(8,128)(2,1)S(1)}, u32[]{:S(2)}, u32[]{:S(2)}) collective-permute-start(bf16[384,2304]{1,0:T(8,128)(2,1)} %bitcast.4), channel_id=1, source_target_pairs={{0,16},{1,17},{2,18},{3,19},{4,20},{5,21},{6,22},{7,23},{8,24},{9,... | collective-permute-start | bytes 5308424 | tf_op jit(solution)/shard_map/ppermute | solution.py:24
  30.0 0.0 copy-done.4
  30.0 128.3 %collective-permute-done.1.incoming_ref = bf16[384,2304]{1,0:T(8,128)(2,1)S(1)} collective-permute-done((bf16[384,2304]{1,0:T(8,128)(2,1)}, bf16[384,2304]{1,0:T(8,128)(2,1)S(1)}, u32[]{:S(2)}, u32[]{:S(2)}) %collective-permute-start.1) | collective-permute-done | bytes 1769504 | tf_op jit(solution)/shard_map/ppermute | solution.py:24
  158.3 0.4 fusion
  158.7 0.5 fusion.2
  159.2 7.1 %collective-permute-start.2 = (bf16[384,2304]{1,0:T(8,128)(2,1)S(1)}, bf16[384,2304]{1,0:T(8,128)(2,1)S(1)}, u32[]{:S(2)}, u32[]{:S(2)}) collective-permute-start(bf16[384,2304]{1,0:T(8,128)(2,1)S(1)} %fusion.2), channel_id=1, source_target_pairs={{0,1},{1,0},{2,3},{3,2},{4,5},{5,4},{6,7},{7,6},{8,9},{9,8},{10,11... | collective-permute-start | bytes 5308424 | tf_op jit(solution)/shard_map/ppermute | solution.py:24
  166.4 0.7 fusion.13
  167.1 0.4 pad_maximum_fusion.3
  167.5 2.2 collective-permute-done.2
  169.7 2.1 pad_maximum_fusion.normed_ref
  171.7 145.3 %all-gather.3.cloned.1.call-done = bf16[1536,2304]{1,0:T(8,128)(2,1)} async-done(((bf16[192,2304]{1,0:T(8,128)(2,1)}), bf16[1536,2304]{1,0:T(8,128)(2,1)}) %all-gather.3.cloned.1.call-update) | async-done | bytes 7077904 | tf_op jit(solution)/shard_map/all_gather | solution.py:246
  317.0 3.1 shard_map.66.mine_ref
  320.1 2.4 collective-permute-start.4
  322.5 0.0 copy-start.1
  322.5 2.0 copy-done.1
  324.5 9.5 %shard_map.64 = (bf16[2,384,256]{2,1,0:T(8,128)(2,1)S(1)}, f32[384,1024]{1,0:T(8,128)S(1)}) custom-call(bf16[768,2304]{1,0:T(8,128)(2,1)S(1)} %copy-done.1, bf16[8,192,2304]{2,1,0:T(8,128)(2,1)} %bitcast.7, f32[384,128]{1,0:T(8,128)S(1)} %get-tuple-element.13.cosine_ref, f32[384,128]{1,0:T(8,128)S(1)} %get-tuple-element.14.sine_ref), custom_call_target="tpu_custom_call" | custom-call | flops 3925868544 | bytes 8257536 | tf_op jit(solution)/shard_map/pallas_call | solution.py:268
  334.0 2.1 collective-permute-start.3
  336.1 0.0 copy-start
  336.1 0.0 copy-start.2
  336.1 3.9 %shard_map.65.here_ref = bf16[2,384,256]{2,1,0:T(8,128)(2,1)S(1)} custom-call(f32[384,1024]{1,0:T(8,128)S(1)} %get-tuple-element.15.raw_ref, f32[384,128]{1,0:T(8,128)S(1)} %get-tuple-element.13.cosine_ref, f32[384,128]{1,0:T(8,128)S(1)} %get-tuple-element.14.sine_ref), custom_call_target="tpu_custom_call" | custom-call | flops 301989888 | tf_op jit(solution)/shard_map/pallas_call | solution.py:281
  340.1 0.0 collective-permute-done.3.there_ref
  340.1 0.0 collective-permute-done.4.theirs_ref
  340.1 0.0 copy-done
  340.1 0.0 copy-done.2
  340.1 3.9 %shard_map.67 = bf16[384,2304]{1,0:T(8,128)(2,1)} custom-call(bf16[2,384,256]{2,1,0:T(8,128)(2,1)S(1)} %shard_map.65.here_ref, bf16[2,384,256]{2,1,0:T(8,128)(2,1)S(1)} %collective-permute-done.3.there_ref, bf16[512,2304]{1,0:T(8,128)(2,1)S(1)} %copy-done, bf16[512,2304]{1,0:T(8,128)(2,1)S(1)} %collective-permute-done.4.theirs_ref, ...), custom_call_target="tpu_custom_call" | custom-call | flops 1811939328 | bytes 8257536 | tf_op jit(solution)/shard_map/pallas_call | solution.py:289
  (5 shorter events, 0.1 us)
Async XLA Ops:
  6.5 310.5 %all-gather.3.cloned.1.call-start = ((), (), s32[]{:S(2)}) async-start(), calls=%async_computation | async-start | bytes 7962624 | tf_op jit(solution)/shard_map/all_gather | solution.py:246
  7.6 11.3 %copy-start.3 = (bf16[1,64,2304]{2,1,0:T(8,128)(2,1)S(1)}, bf16[1,64,2304]{2,1,0:T(8,128)(2,1)}, u32[]{:S(2)}) copy-start(bf16[1,64,2304]{2,1,0:T(8,128)(2,1)} %param.11) | copy-start | bytes 884740
  8.7 10.0 %collective-permute-start = (bf16[144,1024]{1,0:T(8,128)(2,1)S(1)}, bf16[144,1024]{1,0:T(8,128)(2,1)S(1)}, u32[]{:S(2)}, u32[]{:S(2)}) collective-permute-start(bf16[144,1024]{1,0:T(8,128)(2,1)S(1)} %broadcast_select_fusion.2), channel_id=1, source_target_pairs={{0,1},{1,0},{2,3},{3,2},{4,5},{5,4},{6,7},{7,6},{8,9},{9,8},{10,11... | collective-permute-start | bytes 884744 | tf_op jit(solution)/shard_map/ppermute | solution.py:24
  18.8 11.1 %copy-start.4 = (f32[1,2304]{1,0:T(1,128)S(1)}, f32[1,2304]{1,0:T(1,128)}, u32[]{:S(2)}) copy-start(f32[1,2304]{1,0:T(1,128)} %param.7) | copy-start | bytes 27652
  19.9 138.4 %collective-permute-start.1 = (bf16[384,2304]{1,0:T(8,128)(2,1)}, bf16[384,2304]{1,0:T(8,128)(2,1)S(1)}, u32[]{:S(2)}, u32[]{:S(2)}) collective-permute-start(bf16[384,2304]{1,0:T(8,128)(2,1)} %bitcast.4), channel_id=1, source_target_pairs={{0,16},{1,17},{2,18},{3,19},{4,20},{5,21},{6,22},{7,23},{8,24},{9,... | collective-permute-start | bytes 5308424 | tf_op jit(solution)/shard_map/ppermute | solution.py:24
  159.2 10.4 %collective-permute-start.2 = (bf16[384,2304]{1,0:T(8,128)(2,1)S(1)}, bf16[384,2304]{1,0:T(8,128)(2,1)S(1)}, u32[]{:S(2)}, u32[]{:S(2)}) collective-permute-start(bf16[384,2304]{1,0:T(8,128)(2,1)S(1)} %fusion.2), channel_id=1, source_target_pairs={{0,1},{1,0},{2,3},{3,2},{4,5},{5,4},{6,7},{7,6},{8,9},{9,8},{10,11... | collective-permute-start | bytes 5308424 | tf_op jit(solution)/shard_map/ppermute | solution.py:24
  320.1 20.0 %collective-permute-start.4 = (bf16[512,2304]{1,0:T(8,128)(2,1)}, bf16[512,2304]{1,0:T(8,128)(2,1)S(1)}, u32[]{:S(2)}, u32[]{:S(2)}) collective-permute-start(bf16[512,2304]{1,0:T(8,128)(2,1)} %shard_map.66.mine_ref), channel_id=1, source_target_pairs={{0,1},{1,0},{2,3},{3,2},{4,5},{5,4},{6,7},{7,6},{8,9},{9,8},{10,11... | collective-permute-start | bytes 7077896 | tf_op jit(solution)/shard_map/ppermute | solution.py:24
  322.5 2.0 copy-start.1
  334.0 6.1 %collective-permute-start.3 = (bf16[2,384,256]{2,1,0:T(8,128)(2,1)S(1)}, bf16[2,384,256]{2,1,0:T(8,128)(2,1)S(1)}, u32[]{:S(2)}, u32[]{:S(2)}) collective-permute-start(bf16[2,384,256]{2,1,0:T(8,128)(2,1)S(1)} %get-tuple-element.16), channel_id=1, source_target_pairs={{0,1},{1,0},{2,3},{3,2},{4,5},{5,4},{6,7},{7,6},{8,9},{9,8},{10,11... | collective-permute-start | bytes 1179656 | tf_op jit(solution)/shard_map/ppermute | solution.py:24
  336.1 4.0 %copy-start = (bf16[512,2304]{1,0:T(8,128)(2,1)S(1)}, bf16[512,2304]{1,0:T(8,128)(2,1)}, u32[]{:S(2)}) copy-start(bf16[512,2304]{1,0:T(8,128)(2,1)} %shard_map.66.mine_ref) | copy-start | bytes 7077892
  336.1 4.0 %copy-start.2 = (f32[1,2304]{1,0:T(1,128)S(1)}, f32[1,2304]{1,0:T(1,128)}, u32[]{:S(2)}) copy-start(f32[1,2304]{1,0:T(1,128)} %gain_ref.1) | copy-start | bytes 27652
Sparse Core Ops, SparseCore 0:
  20.0 296.9 all-gather.2
